TPU v7x, 1024 devices: a whole 4x4x32 slice. The times are simulated.
1024 devices in a mesh: rep: 8 (over z_lo), node: 8 (over z_hi, core), shard: 16 (over x, y).
Axes of the slice: x: 4, y: 4, z: 32 (z_hi: 4, z_lo: 8; z = z_hi * 8 + z_lo), core: 2. Of those that a mesh axis runs over, the one named last changes fastest.
Arguments:
- hidden_in: bfloat16 [131072, 768], P(('rep', 'node', 'shard')), may hold values from -6 to 6
- expert_ids: int32 [131072, 1], P(('rep', 'node', 'shard')), may hold values from 0 to 7; in each aligned block of 128 rows (0 to 127, 128 to 255, ...) at most 24 rows name the same one
- gate_prob: float32 [131072], P(('rep', 'node', 'shard')), may hold values from 0.1 to 1
- out_grad: bfloat16 [131072, 2048], P(('rep', 'node', 'shard')), may hold values from -24 to 24
- codes: bfloat16 [8, 768, 2048], P('node', None, 'shard'), may hold values from -4 to 4
- scales: float32 [8, 768], P('node'), may hold values from 0.010825317 to 0.10825317
Outputs:
- mixed: bfloat16 [131072, 2048], P(('rep', 'node', 'shard'))
- hidden_grad: bfloat16 [131072, 768], P(('rep', 'node', 'shard'))
- code_grad: float32 [8, 768, 2048], P('node', 'rep', 'shard')
Inputs may be any that keep to these rules, and one draw needn't show every extreme that they name: `expert_ids`: no expert is chosen by more than 24 tokens of one device; that many is reached on some device.
All inputs are finite; a program needn't handle non-finite values.
Results may differ from a plain program's by a relative error of at most 0.022.
Values may be sent and summed in bfloat16 or wider, within the bound.
A program may use at most 32 MiB of HBM per device.

v0:
```python
import jax
import jax.numpy as jnp
from jax import lax
from jax.sharding import PartitionSpec as P


def body(hidden_in, expert_ids, gate_prob, out_grad, codes, scales):
    tok_rows = hidden_in.shape[0]
    flight = lax.axis_size("node")
    per_expert = 3 * tok_rows // (2 * flight)
    slot_count = flight * per_expert
    chosen = expert_ids[:, 0]
    onehot = (chosen[:, None] == jnp.arange(flight, dtype=jnp.int32)[None, :]).astype(jnp.int32)
    rank = jnp.sum(jnp.cumsum(onehot, axis=0) * onehot, axis=1) - 1
    target = chosen * per_expert + rank
    placing = (jnp.arange(slot_count, dtype=jnp.int32)[:, None] == target[None, :]).astype(
        jnp.bfloat16
    )
    scaled = (gate_prob[:, None] * out_grad.astype(jnp.float32)).astype(jnp.bfloat16)
    send_hidden = jnp.dot(placing, hidden_in, preferred_element_type=jnp.float32).astype(
        jnp.bfloat16
    )
    send_scaled = jnp.dot(placing, scaled, preferred_element_type=jnp.float32).astype(jnp.bfloat16)
    send_hidden = send_hidden.reshape(flight, per_expert, send_hidden.shape[1])
    send_scaled = send_scaled.reshape(flight, per_expert, send_scaled.shape[1])
    recv_hidden, recv_scaled = (
        lax.all_to_all(send_hidden, "node", split_axis=0, concat_axis=0, tiled=True),
        lax.all_to_all(send_scaled, "node", split_axis=0, concat_axis=0, tiled=True),
    )
    gathered = lax.all_gather(codes, "shard", axis=2, tiled=True)
    weight = (gathered[0].astype(jnp.float32) * scales[0][:, None]).astype(jnp.bfloat16)
    rows_hidden = recv_hidden.reshape(slot_count, recv_hidden.shape[2])
    rows_scaled = recv_scaled.reshape(slot_count, recv_scaled.shape[2])
    expert_out = jnp.dot(rows_hidden, weight, preferred_element_type=jnp.float32).astype(
        jnp.bfloat16
    )
    back_rows = lax.dot_general(
        rows_scaled, weight, (((1,), (1,)), ((), ())), preferred_element_type=jnp.float32
    ).astype(jnp.bfloat16)
    term = lax.dot_general(
        rows_hidden, rows_scaled, (((0,), (0,)), ((), ())), preferred_element_type=jnp.float32
    )
    returned_out, returned_back = (
        lax.all_to_all(
            expert_out.reshape(flight, per_expert, expert_out.shape[1]),
            "node",
            split_axis=0,
            concat_axis=0,
            tiled=True,
        ),
        lax.all_to_all(
            back_rows.reshape(flight, per_expert, back_rows.shape[1]),
            "node",
            split_axis=0,
            concat_axis=0,
            tiled=True,
        ),
    )
    token_out = lax.dot_general(
        placing,
        returned_out.reshape(slot_count, returned_out.shape[2]),
        (((0,), (0,)), ((), ())),
        preferred_element_type=jnp.float32,
    )
    mixed = (gate_prob[:, None] * token_out).astype(jnp.bfloat16)
    hidden_grad = lax.dot_general(
        placing,
        returned_back.reshape(slot_count, returned_back.shape[2]),
        (((0,), (0,)), ((), ())),
        preferred_element_type=jnp.float32,
    ).astype(jnp.bfloat16)
    partial_cols = lax.psum_scatter(
        term.astype(jnp.bfloat16), "shard", scatter_dimension=1, tiled=True
    )
    owned = lax.psum_scatter(partial_cols, "rep", scatter_dimension=0, tiled=True).astype(
        jnp.float32
    )
    row_count = owned.shape[0]
    row_start = lax.axis_index("rep") * row_count
    row_scales = lax.dynamic_slice_in_dim(scales[0], row_start, row_count, 0)
    code_grad = (owned * row_scales[:, None])[None]
    return (mixed, hidden_grad, code_grad)


def solution(mesh):
    return jax.shard_map(
        body,
        mesh=mesh,
        in_specs=(
            P(("rep", "node", "shard"), None),
            P(("rep", "node", "shard"), None),
            P(("rep", "node", "shard")),
            P(("rep", "node", "shard"), None),
            P("node", None, "shard"),
            P("node", None),
        ),
        out_specs=(
            P(("rep", "node", "shard"), None),
            P(("rep", "node", "shard"), None),
            P("node", "rep", "shard"),
        ),
        check_vma=False,
    )
```

profile of v0, /device:TPU:4, one launch (start us, length us, event | category | flops | bytes accessed | tf_op | source)
XLA Modules:
  0.0 384.3 jit_solution(9654097220030296714)
XLA Ops:
  7.2 0.0 copy-start
  7.2 0.0 copy-start.4
  7.2 0.8 fusion.9
  8.0 0.2 reduce_window_sum.11
  8.1 0.8 select_reduce_fusion
  9.0 0.7 add_add_fusion
  9.6 2.4 convolution_convert_fusion.1
  12.0 28.3 %all-to-all-start.2 = ((bf16[8,24,2048]{2,1,0:T(8,128)(2,1)}), bf16[8,24,2048]{2,1,0:T(8,128)(2,1)S(1)}, u32[]{:S(2)}, u32[]{:S(2)}) async-start(bf16[8,24,2048]{2,1,0:T(8,128)(2,1)} %bitcast.6), calls=%async_computation.2 | async-start | bytes 1572864 | tf_op jit(solution)/shard_map/all_to_all | solution.py:28
  40.4 0.0 all-gather.2.cloned.1.call-start
  40.4 0.7 all-gather.2.cloned.1.call-update
  41.1 0.0 copy-done
  41.1 0.9 convolution_convert_fusion.2
  42.0 83.1 %all-to-all-done.2 = bf16[8,24,2048]{2,1,0:T(8,128)(2,1)S(1)} async-done(((bf16[8,24,2048]{2,1,0:T(8,128)(2,1)}), bf16[8,24,2048]{2,1,0:T(8,128)(2,1)S(1)}, u32[]{:S(2)}, u32[]{:S(2)}) %all-to-all-start.2) | async-done | bytes 786464 | tf_op jit(solution)/shard_map/all_to_all | solution.py:28
  125.1 0.0 copy-start.1
  125.1 6.3 %all-to-all-start = ((bf16[8,24,768]{2,1,0:T(8,128)(2,1)}), bf16[8,24,768]{2,1,0:T(8,128)(2,1)S(1)}, u32[]{:S(2)}, u32[]{:S(2)}) async-start(bf16[8,24,768]{2,1,0:T(8,128)(2,1)} %bitcast.1), calls=%async_computation | async-start | bytes 589824 | tf_op jit(solution)/shard_map/all_to_all | solution.py:27
  131.5 0.0 copy-done.4
  131.5 1.6 all-gather.2.cloned.1.call-done
  133.0 3.9 %fusion.5 = bf16[192,768]{1,0:T(8,128)(2,1)} fusion(bf16[192,2048]{1,0:T(8,128)(2,1)S(1)} %bitcast.33, bf16[1,768,2048]{2,1,0:T(8,128)(2,1)} %all-gather.2.cloned.1.call-done, f32[768]{0:T(1024)S(1)} %reduce), kind=kOutput, calls=%fused_computation.8 | convolution fusion | flops 608845824 | bytes 4230144 | tf_op jit(solution)/shard_map/dot_general | solution.py:37
  136.9 0.0 copy-done.1
  136.9 28.8 %all-to-all-done = bf16[8,24,768]{2,1,0:T(8,128)(2,1)S(1)} async-done(((bf16[8,24,768]{2,1,0:T(8,128)(2,1)}), bf16[8,24,768]{2,1,0:T(8,128)(2,1)S(1)}, u32[]{:S(2)}, u32[]{:S(2)}) %all-to-all-start) | async-done | bytes 294944 | tf_op jit(solution)/shard_map/all_to_all | solution.py:27
  165.7 0.0 copy-start.2
  165.7 14.0 %all-to-all-start.3 = ((bf16[8,24,768]{2,1,0:T(8,128)(2,1)}), bf16[8,24,768]{2,1,0:T(8,128)(2,1)}, u32[]{:S(2)}, u32[]{:S(2)}) async-start(bf16[8,24,768]{2,1,0:T(8,128)(2,1)} %bitcast.8), calls=%async_computation.3 | async-start | bytes 589824 | tf_op jit(solution)/shard_map/all_to_all | solution.py:51
  179.7 0.0 copy-done.2
  179.8 0.0 reduce-scatter.7.cloned.1.call-start
  179.8 2.2 bitcast_convert_fusion
  182.1 2.8 copy.9
  184.9 0.0 copy-start.3
  184.9 0.0 reduce-scatter.7.cloned.1.call-update
  184.9 0.9 copy-done.3
  185.8 0.0 copy-start.5
  185.8 3.7 convolution_convert_fusion
  189.5 26.2 %all-to-all-done.3 = bf16[8,24,768]{2,1,0:T(8,128)(2,1)} async-done(((bf16[8,24,768]{2,1,0:T(8,128)(2,1)}), bf16[8,24,768]{2,1,0:T(8,128)(2,1)}, u32[]{:S(2)}, u32[]{:S(2)}) %all-to-all-start.3) | async-done | bytes 294944 | tf_op jit(solution)/shard_map/all_to_all | solution.py:51
  215.7 10.5 %all-to-all-start.1 = ((bf16[8,24,2048]{2,1,0:T(8,128)(2,1)}), bf16[8,24,2048]{2,1,0:T(8,128)(2,1)S(1)}, u32[]{:S(2)}, u32[]{:S(2)}) async-start(bf16[8,24,2048]{2,1,0:T(8,128)(2,1)} %bitcast.4), calls=%async_computation.1 | async-start | bytes 1572864 | tf_op jit(solution)/shard_map/all_to_all | solution.py:44
  226.1 0.0 reduce-scatter.5.cloned.1.call-start
  226.2 0.1 dynamic-slice_bitcast_fusion
  226.3 72.9 %reduce-scatter.7.cloned.1.call-done = bf16[128,768]{1,0:T(8,128)(2,1)} async-done(((bf16[2048,768]{1,0:T(8,128)(2,1)}), bf16[128,768]{1,0:T(8,128)(2,1)}) %reduce-scatter.7.cloned.1.call-update) | async-done | bytes 196624
  299.2 1.7 copy.10
  300.9 0.0 reduce-scatter.5.cloned.1.call-update
  300.9 1.9 convolution_convert_fusion.3
  302.8 0.0 all-to-all-done.1
  302.8 0.0 copy-done.5
  302.8 1.2 fusion.1
  304.0 72.3 %reduce-scatter.5.cloned.1.call-done = bf16[96,128]{1,0:T(8,128)(2,1)} async-done(((bf16[768,128]{1,0:T(8,128)(2,1)}), bf16[96,128]{1,0:T(8,128)(2,1)}) %reduce-scatter.5.cloned.1.call-update) | async-done | bytes 24592 | tf_op jit(solution)/shard_map/reduce_scatter | solution.py:75
  376.3 1.4 multiply_bitcast_fusion
  (1 shorter events, 0.0 us)
Async XLA Ops:
  7.2 33.9 %copy-start = (bf16[128,768]{1,0:T(8,128)(2,1)S(1)}, bf16[128,768]{1,0:T(8,128)(2,1)}, u32[]{:S(2)}) copy-start(bf16[128,768]{1,0:T(8,128)(2,1)} %param.6) | copy-start | bytes 589828
  7.2 124.3 %copy-start.4 = (f32[1,768]{1,0:T(1,128)S(1)}, f32[1,768]{1,0:T(1,128)}, u32[]{:S(2)}) copy-start(f32[1,768]{1,0:T(1,128)} %param.11) | copy-start | bytes 9220
  12.0 113.1 %all-to-all-start.2 = ((bf16[8,24,2048]{2,1,0:T(8,128)(2,1)}), bf16[8,24,2048]{2,1,0:T(8,128)(2,1)S(1)}, u32[]{:S(2)}, u32[]{:S(2)}) async-start(bf16[8,24,2048]{2,1,0:T(8,128)(2,1)} %bitcast.6), calls=%async_computation.2 | async-start | bytes 1572864 | tf_op jit(solution)/shard_map/all_to_all | solution.py:28
  40.4 92.7 %all-gather.2.cloned.1.call-start = ((), (), s32[]{:S(2)}) async-start(), calls=%async_computation.6 | async-start | bytes 3342336 | tf_op jit(solution)/shard_map/all_gather | solution.py:30
  125.1 11.8 %copy-start.1 = (bf16[8,24,2048]{2,1,0:T(8,128)(2,1)}, bf16[8,24,2048]{2,1,0:T(8,128)(2,1)S(1)}, u32[]{:S(2)}) copy-start(bf16[8,24,2048]{2,1,0:T(8,128)(2,1)S(1)} %all-to-all-done.2) | copy-start | bytes 2359300
  125.1 40.6 %all-to-all-start = ((bf16[8,24,768]{2,1,0:T(8,128)(2,1)}), bf16[8,24,768]{2,1,0:T(8,128)(2,1)S(1)}, u32[]{:S(2)}, u32[]{:S(2)}) async-start(bf16[8,24,768]{2,1,0:T(8,128)(2,1)} %bitcast.1), calls=%async_computation | async-start | bytes 589824 | tf_op jit(solution)/shard_map/all_to_all | solution.py:27
  165.7 14.0 %copy-start.2 = (bf16[8,24,768]{2,1,0:T(8,128)(2,1)}, bf16[8,24,768]{2,1,0:T(8,128)(2,1)S(1)}, u32[]{:S(2)}) copy-start(bf16[8,24,768]{2,1,0:T(8,128)(2,1)S(1)} %all-to-all-done) | copy-start | bytes 884740
  165.7 50.0 %all-to-all-start.3 = ((bf16[8,24,768]{2,1,0:T(8,128)(2,1)}), bf16[8,24,768]{2,1,0:T(8,128)(2,1)}, u32[]{:S(2)}, u32[]{:S(2)}) async-start(bf16[8,24,768]{2,1,0:T(8,128)(2,1)} %bitcast.8), calls=%async_computation.3 | async-start | bytes 589824 | tf_op jit(solution)/shard_map/all_to_all | solution.py:51
  179.8 119.4 %reduce-scatter.7.cloned.1.call-start = ((), (), s32[]{:S(2)}) async-start(), calls=%async_computation.8 | async-start | bytes 3342336
  184.9 1.0 copy-start.3
  185.8 117.0 %copy-start.5 = (f32[128]{0:T(128)S(1)}, f32[128]{0:T(128)}, u32[]{:S(2)}) copy-start(f32[128]{0:T(128)} %param.8) | copy-start | bytes 1540
  215.7 87.1 %all-to-all-start.1 = ((bf16[8,24,2048]{2,1,0:T(8,128)(2,1)}), bf16[8,24,2048]{2,1,0:T(8,128)(2,1)S(1)}, u32[]{:S(2)}, u32[]{:S(2)}) async-start(bf16[8,24,2048]{2,1,0:T(8,128)(2,1)} %bitcast.4), calls=%async_computation.1 | async-start | bytes 1572864 | tf_op jit(solution)/shard_map/all_to_all | solution.py:44
  226.1 150.2 %reduce-scatter.5.cloned.1.call-start = ((), (), s32[]{:S(2)}) async-start(), calls=%async_computation.7 | async-start | bytes 221184 | tf_op jit(solution)/shard_map/reduce_scatter | solution.py:75
Sparse Core Ops, SparseCore 0:
  45.3 87.6 all-gather.1
  186.0 113.1 reduce-scatter.6
  302.6 73.7 reduce-scatter.4
where the time goes:
time: 385 us; the launch traced here: 384 us
  waiting for transfers between devices  286 us (74%)
  starting transfers between devices  59.2 us (15%)
  matrix products  16.2 us (4%)
  between operations  13.8 us (4%)
  local copies, waits for them, and re-layouts  5.6 us (1%)
  other arithmetic  3.89 us (1%)
    all_to_all x1, waiting for transfers between devices, body(): lax.all_to_all(send_scaled, 'node', split_axis=0, concat_axis=0, tiled=True)  83.1 us
    unnamed x4, waiting for transfers between devices  73.6 us
    reduce_scatter x1, waiting for transfers between devices, body(): lax.psum_scatter(partial_cols, 'rep', scatter_dimension=0, tiled=True)  72.3 us
    all_to_all x1, waiting for transfers between devices, body(): lax.all_to_all(send_hidden, 'node', split_axis=0, concat_axis=0, tiled=True)  28.8 us
    all_to_all x1, starting transfers between devices, body(): lax.all_to_all(send_scaled, 'node', split_axis=0, concat_axis=0, tiled=True)  28.3 us
    all_to_all x1, waiting for transfers between devices, body(): lax.all_to_all(back_rows.reshape(flight, per_expert, back_rows.shape[1]),...  26.2 us
    all_to_all x1, starting transfers between devices, body(): lax.all_to_all(back_rows.reshape(flight, per_expert, back_rows.shape[1]),...  14 us
    all_to_all x1, starting transfers between devices, body(): lax.all_to_all(expert_out.reshape(flight, per_expert, expert_out.shape[1]...  10.5 us
  transfers between devices with their start and end apart: 7, of which 6 were waited for; matrix products, arithmetic and copies ran while one was open for 5% of the time, Pallas kernels for 0%

commit v1 on v0

v1 whole, which is shorter than its diff:
```python
import functools

import jax
import jax.numpy as jnp
from jax import lax
from jax.experimental import pallas as pl
from jax.experimental.pallas import tpu as pltpu
from jax.sharding import PartitionSpec as P

MESH = pl.DeviceIdType.MESH
BF = jnp.bfloat16
F32 = jnp.float32


def dot(a, b, dims):
    return lax.dot_general(a, b, (dims, ((), ())), preferred_element_type=F32)


def kernel(
    nl, nh, nx, ny,
    ids_ref, gate_ref, hid_ref, og_ref, codes_ref, scales_ref,
    mixed_ref, hg_ref, cg_ref,
    snd, rcv, ret_snd, ret_rcv, w1, wf, tsnd, g1, g2s, g2,
    d_ss, d_rs, r_ss, r_rs, w1_ss, w1_rs, w2_ss, w2_rs, g1_ss, g1_rs, g2_ss, g2_rs,
):
    ne = 2 * nx
    npl = ny * ne
    nz = nh * nl
    tok, fdim = hid_ref.shape
    cap = snd.shape[1]
    fb = fdim // nl
    cb = codes_ref.shape[2]
    dc = nx * cb
    half = nl // 2 - 1

    zl = lax.axis_index("rep")
    node = lax.axis_index("node")
    shard = lax.axis_index("shard")
    h, c = node // 2, node % 2
    x, y = shard // ny, shard % ny
    z = h * nl + zl
    me = y * ne + x * 2 + c

    def dev(xx, yy, zz, cc):
        return (zz % nl, (zz // nl) * 2 + cc, xx * ny + yy)

    def plane(p):
        return dev((p % ne) // 2, p // ne, z, p % 2)

    def w2_delta(hh, dk):
        return dk - half - hh % 2

    def g1_delta(dk):
        return dk - half - c

    barrier = pltpu.get_barrier_semaphore()

    def signal(target):
        pl.semaphore_signal(barrier, inc=1, device_id=target, device_id_type=MESH)

    @pl.loop(1, npl)
    def _(k):
        signal(plane((me + k) % npl))

    @pl.loop(1, nh)
    def _(k):
        signal(dev(x, y, ((h + k) % nh) * nl + zl, c))

    @pl.loop(0, nx * nl)
    def _(i):
        xs, delta = i // nl, w2_delta(x, i % nl)

        @pl.when(jnp.logical_not((xs == x) & (delta == 0)))
        def _():
            signal(dev(xs, y, (z - delta + nz) % nz, c))

    @pl.loop(0, nl)
    def _(dk):
        delta = g1_delta(dk)

        @pl.when(delta != 0)
        def _():
            signal(dev(x, y, (z - delta + nz) % nz, c))

    @pl.loop(0, nh)
    def _(hs):
        @pl.when(jnp.logical_not((hs == h) & (x == h)))
        def _():
            signal(dev(h, y, hs * nl + zl, c))

    ids = ids_ref[...]
    erows = lax.broadcasted_iota(jnp.int32, (16, tok), 0)
    onehot = (erows == ids).astype(F32)
    ti = lax.broadcasted_iota(jnp.int32, (tok, tok), 0)
    tj = lax.broadcasted_iota(jnp.int32, (tok, tok), 1)
    upto = (ti <= tj).astype(BF)
    count = dot(onehot.astype(BF), upto, ((1,), (0,)))
    rank = jnp.sum(count * onehot, axis=0, keepdims=True) - 1.0
    target = ids * cap + rank.astype(jnp.int32)
    slots = lax.broadcasted_iota(jnp.int32, (ne * cap, tok), 0)
    placing = (slots == target).astype(BF)
    gate = jnp.sum(jnp.where(ti == tj, gate_ref[...], 0.0), axis=1, keepdims=True)

    fi = lax.broadcasted_iota(jnp.int32, (fb, fdim), 0) + zl * fb
    fj = lax.broadcasted_iota(jnp.int32, (fb, fdim), 1)
    scale = jnp.sum(jnp.where(fi == fj, scales_ref[...], 0.0), axis=1, keepdims=True)
    frow = pl.multiple_of(zl * fb, fb)
    block = codes_ref[0, pl.ds(frow, fb), :].astype(F32) * scale
    w1[h] = block.astype(BF)

    pl.semaphore_wait(
        barrier,
        (npl - 1) + (nh - 1) + (nx * nl - 1) + (nl - 1) + nh - jnp.where(x == h, 1, 0),
    )

    def w1_copy(k, slot):
        return pltpu.make_async_remote_copy(
            src_ref=w1.at[slot], dst_ref=w1.at[slot],
            send_sem=w1_ss.at[k], recv_sem=w1_rs.at[slot],
            device_id=dev(x, y, ((h + k) % nh) * nl + zl, c), device_id_type=MESH,
        )

    @pl.loop(1, nh)
    def _(k):
        w1_copy(k, h).start()

    hid_rows = dot(placing, hid_ref[...], ((1,), (0,))).astype(BF).reshape(ne, cap, fdim)
    for yy in range(ny):
        snd[yy * ne:(yy + 1) * ne, :, 0:fdim] = hid_rows
    for yy in range(ny):
        for xx in range(nx):
            s0 = (xx * ny + yy) * cb
            cols = (gate * og_ref[:, s0:s0 + cb].astype(F32)).astype(BF)
            rows = dot(placing, cols, ((1,), (0,))).astype(BF).reshape(ne, cap, cb)
            snd[yy * ne:(yy + 1) * ne, :, fdim + xx * cb:fdim + (xx + 1) * cb] = rows
    rcv[me] = snd[me]

    def d_copy(p, slot):
        return pltpu.make_async_remote_copy(
            src_ref=snd.at[p], dst_ref=rcv.at[slot],
            send_sem=d_ss.at[p], recv_sem=d_rs.at[slot],
            device_id=plane(p), device_id_type=MESH,
        )

    @pl.loop(1, npl)
    def _(k):
        d_copy((me + k) % npl, me).start()

    @pl.loop(1, nh)
    def _(k):
        w1_copy(k, (h + k) % nh).wait_recv()

    wf[pl.ds(frow, fb), pl.ds(pl.multiple_of(x * cb, cb), cb)] = w1[x]

    def w2_copy(hh, delta, fblk, xcol, sem_i, sem_r):
        return pltpu.make_async_remote_copy(
            src_ref=w1.at[hh],
            dst_ref=wf.at[
                pl.ds(pl.multiple_of(fblk * fb, fb), fb), pl.ds(pl.multiple_of(xcol * cb, cb), cb)
            ],
            send_sem=w2_ss.at[sem_i], recv_sem=w2_rs.at[sem_r],
            device_id=dev(hh, y, (z + delta + nz) % nz, c), device_id_type=MESH,
        )

    def w2_not_self(i):
        hh = i // nl
        return jnp.logical_not((hh == x) & (w2_delta(hh, i % nl) == 0))

    @pl.loop(0, nx * nl)
    def _(i):
        @pl.when(w2_not_self(i))
        def _():
            hh = i // nl
            w2_copy(hh, w2_delta(hh, i % nl), zl, x, i, x * nl + zl).start()

    @pl.loop(1, npl)
    def _(k):
        p = (me + k) % npl
        d_copy(p, p).wait_recv()

    sc_all = rcv[:, :, fdim:fdim + dc].reshape(npl * cap, dc)
    fchunk = fdim // 2
    for k in range(2):
        hid_c = rcv[:, :, k * fchunk:(k + 1) * fchunk].reshape(npl * cap, fchunk)
        t = dot(hid_c, sc_all, ((0,), (0,))).astype(BF)
        tsnd[k * (nl // 2):(k + 1) * (nl // 2)] = t.reshape(nl // 2, fb, dc)

    def g1_copy(dk):
        delta = g1_delta(dk)
        return pltpu.make_async_remote_copy(
            src_ref=tsnd.at[(zl + delta + nl) % nl], dst_ref=g1.at[dk],
            send_sem=g1_ss.at[dk], recv_sem=g1_rs.at[dk],
            device_id=dev(x, y, (z + delta + nz) % nz, c), device_id_type=MESH,
        )

    @pl.loop(0, nl)
    def _(dk):
        @pl.when(g1_delta(dk) != 0)
        def _():
            g1_copy(dk).start()

    @pl.loop(0, nx * nl)
    def _(i):
        @pl.when(i != x * nl + zl)
        def _():
            w2_copy(0, 0, i % nl, i // nl, i, i).wait_recv()

    def r_copy(p, slot):
        return pltpu.make_async_remote_copy(
            src_ref=ret_snd.at[p], dst_ref=ret_rcv.at[slot],
            send_sem=r_ss.at[p], recv_sem=r_rs.at[slot],
            device_id=plane(p), device_id_type=MESH,
        )

    @pl.loop(0, ny)
    def _(k):
        p0 = ((y + k) % ny) * ne
        hid_c = rcv[pl.ds(p0, ne), :, 0:fdim].reshape(ne * cap, fdim)
        sc_c = rcv[pl.ds(p0, ne), :, fdim:fdim + dc].reshape(ne * cap, dc)
        o = dot(hid_c, wf[...], ((1,), (0,))).astype(BF)
        ret_snd[pl.ds(p0, ne), :, 0:dc] = o.reshape(ne, cap, dc)
        b = dot(sc_c, wf[...], ((1,), (1,))).astype(BF)
        ret_snd[pl.ds(p0, ne), :, dc:dc + fdim] = b.reshape(ne, cap, fdim)

        @pl.loop(0, ne)
        def _(i):
            p = p0 + (me + i) % ne

            @pl.when(p != me)
            def _():
                r_copy(p, me).start()

    ret_rcv[me] = ret_snd[me]

    @pl.loop(0, nl)
    def _(dk):
        @pl.when(g1_delta(dk) != 0)
        def _():
            g1_copy(dk).wait_recv()

    g1[half + c] = tsnd[zl]
    for j in range(nx):
        part = g1[0, :, j * cb:(j + 1) * cb].astype(F32)
        for dk in range(1, nl):
            part = part + g1[dk, :, j * cb:(j + 1) * cb].astype(F32)
        g2s[j] = part.astype(BF)

    def g2_copy(j, slot):
        return pltpu.make_async_remote_copy(
            src_ref=g2s.at[j], dst_ref=g2.at[slot],
            send_sem=g2_ss.at[j], recv_sem=g2_rs.at[slot],
            device_id=dev(j, y, x * nl + zl, c), device_id_type=MESH,
        )

    @pl.loop(0, nx)
    def _(j):
        @pl.when(jnp.logical_not((j == x) & (x == h)))
        def _():
            g2_copy(j, h).start()

    @pl.when(x == h)
    def _():
        g2[h] = g2s[x]

    @pl.loop(1, npl)
    def _(k):
        p = (me + k) % npl
        r_copy(p, p).wait_recv()

    back = None
    for yy in range(ny):
        rows = ret_rcv[yy * ne:(yy + 1) * ne, :, 0:dc].reshape(ne * cap, dc)
        token_out = gate * dot(placing, rows, ((0,), (0,)))
        for xx in range(nx):
            s0 = (xx * ny + yy) * cb
            mixed_ref[:, s0:s0 + cb] = token_out[:, xx * cb:(xx + 1) * cb].astype(BF)
        part = ret_rcv[yy * ne:(yy + 1) * ne, :, dc:dc + fdim].astype(F32)
        back = part if back is None else back + part
    back = back.reshape(ne * cap, fdim).astype(BF)
    hg_ref[...] = dot(placing, back, ((0,), (0,))).astype(BF)

    @pl.loop(0, nh)
    def _(hs):
        @pl.when(jnp.logical_not((hs == h) & (x == h)))
        def _():
            g2_copy(0, hs).wait_recv()

    total = g2[0].astype(F32)
    for hs in range(1, nh):
        total = total + g2[hs].astype(F32)
    cg_ref[0] = total * scale

    @pl.loop(1, nh)
    def _(k):
        w1_copy(k, h).wait_send()

    @pl.loop(1, npl)
    def _(k):
        p = (me + k) % npl
        d_copy(p, me).wait_send()
        r_copy(p, me).wait_send()

    @pl.loop(0, nx * nl)
    def _(i):
        @pl.when(w2_not_self(i))
        def _():
            w2_copy(0, 0, 0, 0, i, 0).wait_send()

    @pl.loop(0, nl)
    def _(dk):
        @pl.when(g1_delta(dk) != 0)
        def _():
            g1_copy(dk).wait_send()

    @pl.loop(0, nx)
    def _(j):
        @pl.when(jnp.logical_not((j == x) & (x == h)))
        def _():
            g2_copy(j, h).wait_send()


def body(nl, nh, nx, ny, hidden_in, expert_ids, gate_prob, out_grad, codes, scales):
    tok, fdim = hidden_in.shape
    ddim = out_grad.shape[1]
    cb = codes.shape[2]
    dc = nx * cb
    ne = 2 * nx
    npl = ny * ne
    cap = 3 * tok // (2 * ne)
    fb = fdim // nl
    dma = pltpu.SemaphoreType.DMA
    vmem = pl.BlockSpec(memory_space=pltpu.VMEM)
    return pl.pallas_call(
        functools.partial(kernel, nl, nh, nx, ny),
        out_shape=(
            jax.ShapeDtypeStruct((tok, ddim), BF),
            jax.ShapeDtypeStruct((tok, fdim), BF),
            jax.ShapeDtypeStruct((1, fb, cb), F32),
        ),
        in_specs=[vmem] * 6,
        out_specs=(vmem,) * 3,
        scratch_shapes=[
            pltpu.VMEM((npl, cap, fdim + dc), BF),
            pltpu.VMEM((npl, cap, fdim + dc), BF),
            pltpu.VMEM((npl, cap, fdim + dc), BF),
            pltpu.VMEM((npl, cap, fdim + dc), BF),
            pltpu.VMEM((nh, fb, cb), BF),
            pltpu.VMEM((fdim, dc), BF),
            pltpu.VMEM((nl, fb, dc), BF),
            pltpu.VMEM((nl, fb, dc), BF),
            pltpu.VMEM((nx, fb, cb), BF),
            pltpu.VMEM((nh, fb, cb), BF),
            dma((npl,)), dma((npl,)), dma((npl,)), dma((npl,)),
            dma((nh,)), dma((nh,)), dma((nx * nl,)), dma((nx * nl,)),
            dma((nl,)), dma((nl,)), dma((nx,)), dma((nh,)),
        ],
        compiler_params=pltpu.CompilerParams(
            collective_id=0, has_side_effects=True, vmem_limit_bytes=50 * 2**20
        ),
        cost_estimate=pl.CostEstimate(
            flops=6 * npl * cap * fdim * dc, bytes_accessed=4 * tok * ddim, transcendentals=0
        ),
    )(
        expert_ids.reshape(1, tok), gate_prob.reshape(1, tok), hidden_in, out_grad, codes, scales
    )


def solution(mesh):
    nl, nh = mesh.shape["rep"], mesh.shape["node"] // 2
    nx = nh
    ny = mesh.shape["shard"] // nx
    return jax.shard_map(
        functools.partial(body, nl, nh, nx, ny),
        mesh=mesh,
        in_specs=(
            P(("rep", "node", "shard"), None),
            P(("rep", "node", "shard"), None),
            P(("rep", "node", "shard")),
            P(("rep", "node", "shard"), None),
            P("node", None, "shard"),
            P("node", None),
        ),
        out_specs=(
            P(("rep", "node", "shard"), None),
            P(("rep", "node", "shard"), None),
            P("node", "rep", "shard"),
        ),
        check_vma=False,
    )
```

time: 385 us -> 126 us (0.33)
  the two profiles are of different devices: /device:TPU:4 before, /device:TPU:23 now
where the time goes in v1:
time: 126 us
  Pallas kernels  119 us (94%)
  local copies, waits for them, and re-layouts  6.31 us (5%)
    pallas_call x1, Pallas kernels, body(): pl.pallas_call(functools.partial(kernel, nl, nh, nx, ny), out_shape=(jax....  119 us
    unnamed x15, local copies, waits for them, and re-layouts  6.31 us

profile of v1, /device:TPU:23, one launch (start us, length us, event | category | flops | bytes accessed | tf_op | source)
XLA Modules:
  0.0 125.6 jit_solution(18131802894055561610)
XLA Ops:
  0.6 0.0 copy-start.3
  0.6 0.0 copy-start.4
  0.7 0.7 copy-done.3
  1.3 0.0 copy-done.4
  1.3 0.0 copy-start
  1.3 1.0 copy-done
  2.4 0.0 copy-start.1
  2.4 0.9 copy-done.1
  3.3 0.0 copy-start.2
  3.3 0.9 copy-done.2
  4.2 0.0 copy-start.5
  4.2 0.7 copy-done.5
  4.9 118.7 %shard_map.85 = (bf16[128,2048]{1,0:T(8,128)(2,1)S(1)}, bf16[128,768]{1,0:T(8,128)(2,1)S(1)}, f32[1,96,128]{2,1,0:T(8,128)S(1)}) custom-call(s32[1,128]{1,0:T(1,128)S(1)} %bitcast.2, f32[1,128]{1,0:T(1,128)S(1)} %bitcast.3, bf16[128,768]{1,0:T(8,128)(2,1)S(1)} %copy-done.1, bf16[128,2048]{1,0:T(8,128)(2,1)S(1)} %copy-done, ...), custom_call_target="tpu_custom_call" | custom-call | flops 1811939328 | bytes 1048576 | tf_op jit(solution)/shard_map/pallas_call | solution.py:333
  123.5 0.8 copy.12
  124.3 0.7 copy.13
  125.0 0.6 copy.14
Async XLA Ops:
  0.6 0.7 copy-start.3
  0.6 0.7 copy-start.4
  1.3 1.0 copy-start
  2.4 0.9 copy-start.1
  3.3 0.9 copy-start.2
  4.2 0.7 copy-start.5

commit v2 on v1

v2 whole, which is shorter than its diff:
```python
import functools

import jax
import jax.numpy as jnp
from jax import lax
from jax.experimental import pallas as pl
from jax.experimental.pallas import tpu as pltpu
from jax.sharding import PartitionSpec as P

MESH = pl.DeviceIdType.MESH
BF = jnp.bfloat16
F32 = jnp.float32


def dot(a, b, dims):
    return lax.dot_general(a, b, (dims, ((), ())), preferred_element_type=F32)


def kernel(
    nl, nh, nx, ny,
    ids_ref, gate_ref, hid_hbm, og_hbm, codes_hbm, scales_ref,
    mixed_ref, hg_ref, cg_ref,
    hid_ref, og_ref, codes_ref,
    snd, rcv, ret_snd, ret_rcv, xb_snd, xb_rcv, w1, wf, tsnd, g1, g2s, ga, gb,
    in_s, d_ss, d_rs, f_ss, f_rs, r_ss, r_rs, x_ss, x_rs,
    w1_ss, w1_rs, w2_ss, w2_rs, g1_ss, g1_rs, ga_ss, ga_rs, gb_ss, gb_rs,
):
    ne = 2 * nx
    npl = ny * ne
    nsame = npl // 2
    nq = ny // 2
    nz = nh * nl
    tok, fdim = hid_ref.shape
    cap = snd.shape[1]
    fb, cb = codes_ref.shape
    dc = nx * cb
    half = nl // 2 - 1

    zl = lax.axis_index("rep")
    node = lax.axis_index("node")
    shard = lax.axis_index("shard")
    h, c = node // 2, node % 2
    x, y = shard // ny, shard % ny
    z = h * nl + zl
    quarter = (y // 2) * 2 + c
    me = quarter * ne + x * 2 + y % 2
    me_same = (quarter // 2) * ne + x * 2 + y % 2
    ty, tc = (y // 2) * 2 + c, y % 2
    untwisted = y % 2 == c

    def dev(xx, yy, zz, cc):
        return (zz % nl, (zz // nl) * 2 + cc, xx * ny + yy)

    def plane(p):
        q, e = p // ne, p % ne
        return dev(e // 2, (q // 2) * 2 + e % 2, z, q % 2)

    def of_core(i, core):
        return ((i // ne) * 2 + core) * ne + i % ne

    def w2_delta(hh, dk):
        return dk - half - hh % 2

    def g1_delta(dk):
        return dk - half - c

    frow = pl.multiple_of(zl * fb, fb)
    loads = (
        pltpu.make_async_copy(codes_hbm.at[0, pl.ds(frow, fb)], codes_ref, in_s.at[0]),
        pltpu.make_async_copy(hid_hbm, hid_ref, in_s.at[1]),
        pltpu.make_async_copy(og_hbm, og_ref, in_s.at[2]),
    )
    for load in loads:
        load.start()

    barrier = pltpu.get_barrier_semaphore()

    def signal(target):
        pl.semaphore_signal(barrier, inc=1, device_id=target, device_id_type=MESH)

    def w2_self(hh, delta):
        return (hh == x) & untwisted & (delta == 0)

    @pl.loop(1, npl)
    def _(k):
        signal(plane((me + k) % npl))

    @pl.loop(1, nh)
    def _(k):
        signal(dev(x, y, ((h + k) % nh) * nl + zl, c))

    @pl.loop(0, nx * nl)
    def _(i):
        xs, delta = i // nl, w2_delta(x, i % nl)

        @pl.when(jnp.logical_not(w2_self(xs, delta)))
        def _():
            signal(dev(xs, ty, (z - delta + nz) % nz, tc))

    @pl.loop(0, nl)
    def _(dk):
        delta = g1_delta(dk)

        @pl.when(delta != 0)
        def _():
            signal(dev(x, y, (z - delta + nz) % nz, c))

    ids = ids_ref[...]
    erows = lax.broadcasted_iota(jnp.int32, (16, tok), 0)
    onehot = (erows == ids).astype(F32)
    ti = lax.broadcasted_iota(jnp.int32, (tok, tok), 0)
    tj = lax.broadcasted_iota(jnp.int32, (tok, tok), 1)
    upto = (ti <= tj).astype(BF)
    count = dot(onehot.astype(BF), upto, ((1,), (0,)))
    rank = jnp.sum(count * onehot, axis=0, keepdims=True) - 1.0
    target = ids * cap + rank.astype(jnp.int32)
    slots = lax.broadcasted_iota(jnp.int32, (ne * cap, tok), 0)
    placing = (slots == target).astype(BF)
    gate = jnp.sum(jnp.where(ti == tj, gate_ref[...], 0.0), axis=1, keepdims=True)

    fi = lax.broadcasted_iota(jnp.int32, (fb, fdim), 0) + zl * fb
    fj = lax.broadcasted_iota(jnp.int32, (fb, fdim), 1)
    scale = jnp.sum(jnp.where(fi == fj, scales_ref[...], 0.0), axis=1, keepdims=True)
    loads[0].wait()
    w1[h] = (codes_ref[...].astype(F32) * scale).astype(BF)

    loads[1].wait()
    hid_rows = dot(placing, hid_ref[...], ((1,), (0,))).astype(BF).reshape(ne, cap, fdim)
    for k in range(nq):
        snd[pl.ds((2 * k + c) * ne, ne), :, 0:fdim] = hid_rows
    loads[2].wait()
    for q in range(ny):
        for xx in range(nx):
            s0 = (xx * ny + q) * cb
            cols = (gate * og_ref[:, s0:s0 + cb].astype(F32)).astype(BF)
            rows = dot(placing, cols, ((1,), (0,))).astype(BF).reshape(ne, cap, cb)
            snd[q * ne:(q + 1) * ne, :, fdim + xx * cb:fdim + (xx + 1) * cb] = rows
    rcv[me] = snd[me]

    pl.semaphore_wait(
        barrier,
        (npl - 1) + (nh - 1) + (nx * nl - jnp.where(untwisted, 1, 0)) + (nl - 1),
    )

    def w1_copy(k, slot):
        return pltpu.make_async_remote_copy(
            src_ref=w1.at[slot], dst_ref=w1.at[slot],
            send_sem=w1_ss.at[k], recv_sem=w1_rs.at[slot],
            device_id=dev(x, y, ((h + k) % nh) * nl + zl, c), device_id_type=MESH,
        )

    @pl.loop(1, nh)
    def _(k):
        w1_copy(k, h).start()

    def d_whole(p, slot):
        return pltpu.make_async_remote_copy(
            src_ref=snd.at[p], dst_ref=rcv.at[slot],
            send_sem=d_ss.at[p], recv_sem=d_rs.at[slot],
            device_id=plane(p), device_id_type=MESH,
        )

    def d_scaled(p, slot):
        return pltpu.make_async_remote_copy(
            src_ref=snd.at[p, :, pl.ds(fdim, dc)], dst_ref=rcv.at[slot, :, pl.ds(fdim, dc)],
            send_sem=d_ss.at[p], recv_sem=d_rs.at[slot],
            device_id=plane(p), device_id_type=MESH,
        )

    def d_forward(i, slot):
        return pltpu.make_async_remote_copy(
            src_ref=rcv.at[slot, :, pl.ds(0, fdim)], dst_ref=rcv.at[slot, :, pl.ds(0, fdim)],
            send_sem=f_ss.at[i], recv_sem=f_rs.at[i],
            device_id=dev(x, y, z, 1 - c), device_id_type=MESH,
        )

    d_forward(me_same, me).start()

    @pl.loop(1, nsame)
    def _(k):
        d_whole(of_core((me_same + k) % nsame, c), me).start()

    @pl.loop(0, nsame)
    def _(k):
        d_scaled(of_core((me_same + k) % nsame, 1 - c), me).start()

    @pl.loop(1, nh)
    def _(k):
        w1_copy(k, (h + k) % nh).wait_recv()

    @pl.when(untwisted)
    def _():
        wf[pl.ds(frow, fb), pl.ds(pl.multiple_of(x * cb, cb), cb)] = w1[x]

    def w2_copy(hh, delta, fblk, xcol, sem_i, sem_r):
        return pltpu.make_async_remote_copy(
            src_ref=w1.at[hh],
            dst_ref=wf.at[
                pl.ds(pl.multiple_of(fblk * fb, fb), fb), pl.ds(pl.multiple_of(xcol * cb, cb), cb)
            ],
            send_sem=w2_ss.at[sem_i], recv_sem=w2_rs.at[sem_r],
            device_id=dev(hh, ty, (z + delta + nz) % nz, tc), device_id_type=MESH,
        )

    @pl.loop(0, nx * nl)
    def _(i):
        hh, delta = i // nl, w2_delta(i // nl, i % nl)

        @pl.when(jnp.logical_not(w2_self(hh, delta)))
        def _():
            w2_copy(hh, delta, zl, x, i, x * nl + zl).start()

    @pl.loop(1, nsame)
    def _(k):
        i = (me_same - k + nsame) % nsame
        p = of_core(i, c)
        d_whole(p, p).wait_recv()
        d_forward(i, p).start()

    @pl.loop(0, nsame)
    def _(k):
        p = of_core((me_same - k + nsame) % nsame, 1 - c)
        d_scaled(p, p).wait_recv()

    @pl.loop(0, nsame)
    def _(i):
        d_forward(i, of_core(i, 1 - c)).wait_recv()

    sc_all = rcv[:, :, fdim:fdim + dc].reshape(npl * cap, dc)
    fchunk = fdim // 2
    for k in range(2):
        hid_c = rcv[:, :, k * fchunk:(k + 1) * fchunk].reshape(npl * cap, fchunk)
        t = dot(hid_c, sc_all, ((0,), (0,))).astype(BF)
        tsnd[k * (nl // 2):(k + 1) * (nl // 2)] = t.reshape(nl // 2, fb, dc)

    def g1_copy(dk):
        delta = g1_delta(dk)
        return pltpu.make_async_remote_copy(
            src_ref=tsnd.at[(zl + delta + nl) % nl], dst_ref=g1.at[dk],
            send_sem=g1_ss.at[dk], recv_sem=g1_rs.at[dk],
            device_id=dev(x, y, (z + delta + nz) % nz, c), device_id_type=MESH,
        )

    @pl.loop(0, nl)
    def _(dk):
        @pl.when(g1_delta(dk) != 0)
        def _():
            g1_copy(dk).start()

    @pl.loop(0, nx * nl)
    def _(i):
        @pl.when(jnp.logical_not(untwisted & (i == x * nl + zl)))
        def _():
            w2_copy(0, 0, i % nl, i // nl, i, i).wait_recv()

    def x_copy(k):
        return pltpu.make_async_remote_copy(
            src_ref=xb_snd.at[k], dst_ref=xb_rcv.at[k],
            send_sem=x_ss.at[k], recv_sem=x_rs.at[k],
            device_id=dev(x, y, z, 1 - c), device_id_type=MESH,
        )

    def r_whole(p, slot):
        return pltpu.make_async_remote_copy(
            src_ref=ret_snd.at[p], dst_ref=ret_rcv.at[slot],
            send_sem=r_ss.at[p], recv_sem=r_rs.at[slot],
            device_id=plane(p), device_id_type=MESH,
        )

    def r_out(p, slot):
        return pltpu.make_async_remote_copy(
            src_ref=ret_snd.at[p, :, pl.ds(0, dc)], dst_ref=ret_rcv.at[slot, :, pl.ds(0, dc)],
            send_sem=r_ss.at[p], recv_sem=r_rs.at[slot],
            device_id=plane(p), device_id_type=MESH,
        )

    @pl.loop(0, nq)
    def _(k):
        p0 = (2 * k + 1 - c) * ne
        sc_c = rcv[pl.ds(p0, ne), :, fdim:fdim + dc].reshape(ne * cap, dc)
        b = dot(sc_c, wf[...], ((1,), (1,))).astype(BF)
        xb_snd[k] = b.reshape(ne, cap, fdim)
        x_copy(k).start()
        hid_c = rcv[pl.ds(p0, ne), :, 0:fdim].reshape(ne * cap, fdim)
        o = dot(hid_c, wf[...], ((1,), (0,))).astype(BF)
        ret_snd[pl.ds(p0, ne), :, 0:dc] = o.reshape(ne, cap, dc)

        @pl.loop(0, ne)
        def _(i):
            r_out(p0 + (me + i) % ne, me).start()

    @pl.loop(0, nq)
    def _(k):
        p0 = (2 * k + c) * ne
        hid_c = rcv[pl.ds(p0, ne), :, 0:fdim].reshape(ne * cap, fdim)
        sc_c = rcv[pl.ds(p0, ne), :, fdim:fdim + dc].reshape(ne * cap, dc)
        o = dot(hid_c, wf[...], ((1,), (0,))).astype(BF)
        ret_snd[pl.ds(p0, ne), :, 0:dc] = o.reshape(ne, cap, dc)
        b = dot(sc_c, wf[...], ((1,), (1,)))
        x_copy(k).wait_recv()
        b = b.reshape(ne, cap, fdim) + xb_rcv[k].astype(F32)
        ret_snd[pl.ds(p0, ne), :, dc:dc + fdim] = b.astype(BF)

        @pl.loop(0, ne)
        def _(i):
            p = p0 + (me + i) % ne

            @pl.when(p != me)
            def _():
                r_whole(p, me).start()

    ret_rcv[me] = ret_snd[me]

    @pl.loop(0, nl)
    def _(dk):
        @pl.when(g1_delta(dk) != 0)
        def _():
            g1_copy(dk).wait_recv()

    g1[half + c] = tsnd[zl]
    for j in range(nx):
        part = g1[0, :, j * cb:(j + 1) * cb].astype(F32)
        for dk in range(1, nl):
            part = part + g1[dk, :, j * cb:(j + 1) * cb].astype(F32)
        g2s[j] = part.astype(BF)

    def ga_copy(j, slot):
        return pltpu.make_async_remote_copy(
            src_ref=g2s.at[j], dst_ref=ga.at[slot],
            send_sem=ga_ss.at[j], recv_sem=ga_rs.at[slot],
            device_id=dev(j, ty, z, tc), device_id_type=MESH,
        )

    def gb_copy(j, slot):
        return pltpu.make_async_remote_copy(
            src_ref=ga.at[j], dst_ref=gb.at[slot],
            send_sem=gb_ss.at[j], recv_sem=gb_rs.at[slot],
            device_id=dev(x, y, j * nl + zl, c), device_id_type=MESH,
        )

    @pl.loop(0, nx)
    def _(j):
        @pl.when(jnp.logical_not((j == x) & untwisted))
        def _():
            ga_copy(j, x).start()

    @pl.when(untwisted)
    def _():
        ga[x] = g2s[x]

    @pl.loop(0, nx)
    def _(j):
        @pl.when(jnp.logical_not((j == x) & untwisted))
        def _():
            ga_copy(j, j).wait_recv()

        @pl.when(j != h)
        def _():
            gb_copy(j, h).start()

    gb[h] = ga[h]

    @pl.loop(0, nsame)
    def _(k):
        p = of_core((me_same - k + nsame) % nsame, 1 - c)
        r_out(p, p).wait_recv()

    @pl.loop(1, nsame)
    def _(k):
        p = of_core((me_same - k + nsame) % nsame, c)
        r_whole(p, p).wait_recv()

    for q in range(ny):
        rows = ret_rcv[q * ne:(q + 1) * ne, :, 0:dc].reshape(ne * cap, dc)
        token_out = gate * dot(placing, rows, ((0,), (0,)))
        for xx in range(nx):
            s0 = (xx * ny + q) * cb
            mixed_ref[:, s0:s0 + cb] = token_out[:, xx * cb:(xx + 1) * cb].astype(BF)
    back = ret_rcv[pl.ds(c * ne, ne), :, dc:dc + fdim].astype(F32)
    for k in range(1, nq):
        back = back + ret_rcv[pl.ds((2 * k + c) * ne, ne), :, dc:dc + fdim].astype(F32)
    back = back.reshape(ne * cap, fdim).astype(BF)
    hg_ref[...] = dot(placing, back, ((0,), (0,))).astype(BF)

    @pl.loop(0, nh)
    def _(hs):
        @pl.when(hs != h)
        def _():
            gb_copy(0, hs).wait_recv()

    total = gb[0].astype(F32)
    for hs in range(1, nh):
        total = total + gb[hs].astype(F32)
    cg_ref[0] = total * scale

    @pl.loop(1, nh)
    def _(k):
        w1_copy(k, h).wait_send()

    @pl.loop(0, nsame)
    def _(i):
        p, far = of_core(i, c), of_core(i, 1 - c)
        d_forward(i, p).wait_send()
        d_scaled(far, me).wait_send()
        r_out(far, me).wait_send()

        @pl.when(p != me)
        def _():
            d_whole(p, me).wait_send()
            r_whole(p, me).wait_send()

    @pl.loop(0, nq)
    def _(k):
        x_copy(k).wait_send()

    @pl.loop(0, nx * nl)
    def _(i):
        @pl.when(jnp.logical_not(w2_self(i // nl, w2_delta(i // nl, i % nl))))
        def _():
            w2_copy(0, 0, 0, 0, i, 0).wait_send()

    @pl.loop(0, nl)
    def _(dk):
        @pl.when(g1_delta(dk) != 0)
        def _():
            g1_copy(dk).wait_send()

    @pl.loop(0, nx)
    def _(j):
        @pl.when(jnp.logical_not((j == x) & untwisted))
        def _():
            ga_copy(j, x).wait_send()

        @pl.when(j != h)
        def _():
            gb_copy(j, h).wait_send()


def body(nl, nh, nx, ny, hidden_in, expert_ids, gate_prob, out_grad, codes, scales):
    tok, fdim = hidden_in.shape
    ddim = out_grad.shape[1]
    cb = codes.shape[2]
    dc = nx * cb
    ne = 2 * nx
    npl = ny * ne
    cap = 3 * tok // (2 * ne)
    fb = fdim // nl
    dma = pltpu.SemaphoreType.DMA
    vmem = pl.BlockSpec(memory_space=pltpu.VMEM)
    hbm = pl.BlockSpec(memory_space=pl.ANY)
    return pl.pallas_call(
        functools.partial(kernel, nl, nh, nx, ny),
        out_shape=(
            jax.ShapeDtypeStruct((tok, ddim), BF),
            jax.ShapeDtypeStruct((tok, fdim), BF),
            jax.ShapeDtypeStruct((1, fb, cb), F32),
        ),
        in_specs=[vmem, vmem, hbm, hbm, hbm, vmem],
        out_specs=(vmem,) * 3,
        scratch_shapes=[
            pltpu.VMEM((tok, fdim), BF),
            pltpu.VMEM((tok, ddim), BF),
            pltpu.VMEM((fb, cb), BF),
            pltpu.VMEM((npl, cap, fdim + dc), BF),
            pltpu.VMEM((npl, cap, fdim + dc), BF),
            pltpu.VMEM((npl, cap, fdim + dc), BF),
            pltpu.VMEM((npl, cap, fdim + dc), BF),
            pltpu.VMEM((ny // 2, ne, cap, fdim), BF),
            pltpu.VMEM((ny // 2, ne, cap, fdim), BF),
            pltpu.VMEM((nh, fb, cb), BF),
            pltpu.VMEM((fdim, dc), BF),
            pltpu.VMEM((nl, fb, dc), BF),
            pltpu.VMEM((nl, fb, dc), BF),
            pltpu.VMEM((nx, fb, cb), BF),
            pltpu.VMEM((nx, fb, cb), BF),
            pltpu.VMEM((nh, fb, cb), BF),
            dma((3,)), dma((npl,)), dma((npl,)), dma((npl // 2,)), dma((npl // 2,)),
            dma((npl,)), dma((npl,)), dma((ny // 2,)), dma((ny // 2,)),
            dma((nh,)), dma((nh,)), dma((nx * nl,)), dma((nx * nl,)),
            dma((nl,)), dma((nl,)), dma((nx,)), dma((nx,)), dma((nx,)), dma((nh,)),
        ],
        compiler_params=pltpu.CompilerParams(
            collective_id=0, has_side_effects=True, vmem_limit_bytes=60 * 2**20
        ),
        cost_estimate=pl.CostEstimate(
            flops=6 * npl * cap * fdim * dc, bytes_accessed=4 * tok * ddim, transcendentals=0
        ),
    )(
        expert_ids.reshape(1, tok), gate_prob.reshape(1, tok), hidden_in, out_grad, codes, scales
    )


def solution(mesh):
    nl, nh = mesh.shape["rep"], mesh.shape["node"] // 2
    nx = nh
    ny = mesh.shape["shard"] // nx
    return jax.shard_map(
        functools.partial(body, nl, nh, nx, ny),
        mesh=mesh,
        in_specs=(
            P(("rep", "node", "shard"), None),
            P(("rep", "node", "shard"), None),
            P(("rep", "node", "shard")),
            P(("rep", "node", "shard"), None),
            P("node", None, "shard"),
            P("node", None),
        ),
        out_specs=(
            P(("rep", "node", "shard"), None),
            P(("rep", "node", "shard"), None),
            P("node", "rep", "shard"),
        ),
        check_vma=False,
    )
```

time: 126 us -> 106 us (0.84)
  the two profiles are of different devices: /device:TPU:23 before, /device:TPU:49 now
where the time goes in v2:
time: 106 us; the launch traced here: 105 us
  Pallas kernels  101 us (95%)
  local copies, waits for them, and re-layouts  3.34 us (3%)
    pallas_call x1, Pallas kernels, body(): pl.pallas_call(functools.partial(kernel, nl, nh, nx, ny), out_shape=(jax....  101 us
    unnamed x7, local copies, waits for them, and re-layouts  3.34 us

profile of v2, /device:TPU:49, one launch (start us, length us, event | category | flops | bytes accessed | tf_op | source)
XLA Modules:
  0.0 105.4 jit_solution(2510647614217326514)
XLA Ops:
  0.6 101.4 %shard_map.85 = (bf16[128,2048]{1,0:T(8,128)(2,1)}, bf16[128,768]{1,0:T(8,128)(2,1)}, f32[1,96,128]{2,1,0:T(8,128)}) custom-call(s32[1,128]{1,0:T(1,128)} %bitcast.2, f32[1,128]{1,0:T(1,128)} %bitcast.3, bf16[128,768]{1,0:T(8,128)(2,1)} %hid_hbm.1, bf16[128,2048]{1,0:T(8,128)(2,1)} %og_hbm.1, bf16[1,768,128]{2,1,0:T(8,128)(2,1)} %codes_hbm.1, ...), custom_call_target="tpu_custom_call" | custom-call | flops 1811939328 | bytes 1048576 | tf_op jit(solution)/shard_map/pallas_call | solution.py:451
  102.0 0.0 copy-start
  102.0 1.9 %copy.12 = bf16[128,2048]{1,0:T(8,128)(2,1)} copy(bf16[128,2048]{1,0:T(8,128)(2,1)} %get-tuple-element.6) | data formatting | bytes 1048576
  103.9 0.0 copy-done
  104.0 0.0 copy-start.1
  104.0 0.7 copy.13
  104.6 0.1 copy-done.1
  104.8 0.6 copy.14
Async XLA Ops:
  102.0 1.9 %copy-start = (bf16[128,768]{1,0:T(8,128)(2,1)S(1)}, bf16[128,768]{1,0:T(8,128)(2,1)}, u32[]{:S(2)}) copy-start(bf16[128,768]{1,0:T(8,128)(2,1)} %get-tuple-element.7) | copy-start | bytes 589828
  104.0 0.8 copy-start.1

commit v3 on v2

v3 whole, which is shorter than its diff:
```python
import functools

import jax
import jax.numpy as jnp
from jax import lax
from jax.experimental import pallas as pl
from jax.experimental.pallas import tpu as pltpu
from jax.sharding import PartitionSpec as P

MESH = pl.DeviceIdType.MESH
BF = jnp.bfloat16
F32 = jnp.float32


def dot(a, b, dims):
    return lax.dot_general(a, b, (dims, ((), ())), preferred_element_type=F32)


def div(a, b):
    return a // b if isinstance(a, int) else lax.div(a, b)


def rem(a, b):
    return a % b if isinstance(a, int) else lax.rem(a, b)


def kernel(
    nl, nh, nx, ny,
    ids_ref, gate_ref, hid_hbm, og_hbm, codes_hbm, scales_ref,
    mixed_ref, hg_ref, cg_ref,
    hid_ref, og_ref, codes_ref,
    snd, rcv, ret_snd, ret_rcv, xb_snd, xb_rcv, wown, w1, wf, tsnd, lng, sht, g2s, ga, gb,
    in_s, d_ss, d_rs, f_ss, f_rs, r_ss, r_rs, x_ss, x_rs,
    w1_ss, w1_rs, wo_ss, wo_rs, w2_ss, w2_rs, lg_ss, lg_rs, sh_ss, sh_rs, ga_ss, ga_rs, gb_ss, gb_rs,
):
    ne = 2 * nx
    npl = ny * ne
    nsame = div(npl, 2)
    nq = div(ny, 2)
    nz = nh * nl
    tok, fdim = hid_ref.shape
    cap = snd.shape[1]
    cb = codes_ref.shape[1]
    fb = div(fdim, nl)
    dc = nx * cb
    hc = div(dc, 2)
    steps = div(nl, 2)

    zl = lax.axis_index("rep")
    node = lax.axis_index("node")
    shard = lax.axis_index("shard")
    h, c = div(node, 2), rem(node, 2)
    x, y = div(shard, ny), rem(shard, ny)
    z = h * nl + zl
    quarter = div(y, 2) * 2 + c
    me = quarter * ne + x * 2 + rem(y, 2)
    me_same = div(quarter, 2) * ne + x * 2 + rem(y, 2)
    ty, tc = div(y, 2) * 2 + c, rem(y, 2)
    untwisted = rem(y, 2) == c

    def dev(xx, yy, zz, cc):
        return (rem(zz, nl), div(zz, nl) * 2 + cc, xx * ny + yy)

    sibling = dev(x, y, z, 1 - c)

    def plane(p):
        q, e = div(p, ne), rem(p, ne)
        return dev(div(e, 2), div(q, 2) * 2 + rem(e, 2), z, rem(q, 2))

    def of_core(i, core):
        return (div(i, ne) * 2 + core) * ne + rem(i, ne)

    def w2_delta(hh, dk):
        return dk - (div(nl, 2) - 1) - rem(hh, 2)

    def w1_turn(k):
        return (2 * c - 1) if 2 * k == nh else 0

    way = 1 - 2 * c

    frow = pl.multiple_of(zl * fb, fb)
    loads = (
        pltpu.make_async_copy(codes_hbm.at[0], codes_ref, in_s.at[0]),
        pltpu.make_async_copy(hid_hbm, hid_ref, in_s.at[1]),
        pltpu.make_async_copy(og_hbm, og_ref, in_s.at[2]),
    )
    for load in loads:
        load.start()

    barrier = pltpu.get_barrier_semaphore()

    def signal(target):
        pl.semaphore_signal(barrier, inc=1, device_id=target, device_id_type=MESH)

    def w2_self(hh, delta):
        return (hh == x) & untwisted & (delta == 0)

    @pl.loop(1, npl)
    def _(k):
        signal(plane(rem(me + k, npl)))

    for k in range(1, nh):
        signal(dev(x, y, rem(h - k + nh, nh) * nl + rem(zl - w1_turn(k) + nl, nl), c))
        signal(dev(x, y, rem(h + k, nh) * nl + zl, c))

    @pl.loop(0, nx * nl)
    def _(i):
        xs, delta = div(i, nl), w2_delta(x, rem(i, nl))

        @pl.when(jnp.logical_not(w2_self(xs, delta)))
        def _():
            signal(dev(xs, ty, rem(z - delta + nz, nz), tc))

    signal(dev(x, y, rem(z + 1, nz), c))
    signal(dev(x, y, rem(z - 1 + nz, nz), c))

    ids = ids_ref[...]
    erows = lax.broadcasted_iota(jnp.int32, (16, tok), 0)
    onehot = (erows == ids).astype(F32)
    ti = lax.broadcasted_iota(jnp.int32, (tok, tok), 0)
    tj = lax.broadcasted_iota(jnp.int32, (tok, tok), 1)
    upto = (ti <= tj).astype(BF)
    count = dot(onehot.astype(BF), upto, ((1,), (0,)))
    rank = jnp.sum(count * onehot, axis=0, keepdims=True) - 1.0
    target = ids * cap + rank.astype(jnp.int32)
    slots = lax.broadcasted_iota(jnp.int32, (ne * cap, tok), 0)
    placing = (slots == target).astype(BF)
    gate = jnp.sum(jnp.where(ti == tj, gate_ref[...], 0.0), axis=1, keepdims=True)

    fi = lax.broadcasted_iota(jnp.int32, (fb, fdim), 0) + zl * fb
    fj = lax.broadcasted_iota(jnp.int32, (fb, fdim), 1)
    scale = jnp.sum(jnp.where(fi == fj, scales_ref[...], 0.0), axis=1, keepdims=True)
    loads[0].wait()
    wide = min(128, fdim)
    eye_r = lax.broadcasted_iota(jnp.int32, (wide, wide), 0)
    eye_c = lax.broadcasted_iota(jnp.int32, (wide, wide), 1)
    for f0 in range(0, fdim, wide):
        col = jnp.where(eye_r == eye_c, scales_ref[:, f0:f0 + wide], 0.0)
        col = jnp.sum(col, axis=1, keepdims=True)
        wown[f0:f0 + wide] = (codes_ref[f0:f0 + wide].astype(F32) * col).astype(BF)
    w1[h] = wown[pl.ds(frow, fb)]

    loads[1].wait()
    hid_rows = dot(placing, hid_ref[...], ((1,), (0,))).astype(BF).reshape(ne, cap, fdim)
    for k in range(nq):
        snd[pl.ds((2 * k + c) * ne, ne), :, 0:fdim] = hid_rows
    loads[2].wait()
    for q in range(ny):
        for xx in range(nx):
            s0 = (xx * ny + q) * cb
            cols = (gate * og_ref[:, s0:s0 + cb].astype(F32)).astype(BF)
            rows = dot(placing, cols, ((1,), (0,))).astype(BF).reshape(ne, cap, cb)
            snd[q * ne:(q + 1) * ne, :, fdim + xx * cb:fdim + (xx + 1) * cb] = rows
    rcv[me] = snd[me]

    pl.semaphore_wait(
        barrier,
        (npl - 1) + 2 * (nh - 1) + (nx * nl - jnp.where(untwisted, 1, 0)) + 2,
    )

    def w1_copy(k, slot):
        row = rem(zl + w1_turn(k) + nl, nl)
        return pltpu.make_async_remote_copy(
            src_ref=wown.at[pl.ds(pl.multiple_of(row * fb, fb), fb)], dst_ref=w1.at[slot],
            send_sem=w1_ss.at[k], recv_sem=w1_rs.at[slot],
            device_id=dev(x, y, rem(h + k, nh) * nl + row, c), device_id_type=MESH,
        )

    def wo_copy(xcol):
        return pltpu.make_async_remote_copy(
            src_ref=wown, dst_ref=wf.at[:, pl.ds(pl.multiple_of(xcol * cb, cb), cb)],
            send_sem=wo_ss, recv_sem=wo_rs.at[xcol],
            device_id=dev(h, ty, z, tc), device_id_type=MESH,
        )

    near_first = sorted(range(1, nh), key=lambda k: -abs(2 * k - nh))
    for k in reversed(near_first):
        w1_copy(k, h).start()

    def d_whole(p, slot, target=None):
        return pltpu.make_async_remote_copy(
            src_ref=snd.at[p], dst_ref=rcv.at[slot],
            send_sem=d_ss.at[p], recv_sem=d_rs.at[slot],
            device_id=target or plane(p), device_id_type=MESH,
        )

    def d_scaled(p, slot, target=None):
        return pltpu.make_async_remote_copy(
            src_ref=snd.at[p, :, pl.ds(fdim, dc)], dst_ref=rcv.at[slot, :, pl.ds(fdim, dc)],
            send_sem=d_ss.at[p], recv_sem=d_rs.at[slot],
            device_id=target or plane(p), device_id_type=MESH,
        )

    def d_forward(i, slot):
        return pltpu.make_async_remote_copy(
            src_ref=rcv.at[slot, :, pl.ds(0, fdim)], dst_ref=rcv.at[slot, :, pl.ds(0, fdim)],
            send_sem=f_ss.at[i], recv_sem=f_rs.at[i],
            device_id=sibling, device_id_type=MESH,
        )

    d_forward(me_same, me).start()

    @pl.loop(1, nsame)
    def _(k):
        d_whole(of_core(rem(me_same + k, nsame), c), me).start()

    @pl.loop(0, nsame)
    def _(k):
        d_scaled(of_core(rem(me_same + k, nsame), 1 - c), me).start()

    @pl.when(jnp.logical_not((x == h) & untwisted))
    def _():
        wo_copy(x).start()

    @pl.when((x == h) & untwisted)
    def _():
        wf[:, pl.ds(pl.multiple_of(x * cb, cb), cb)] = wown[...]

    def w2_copy(hh, delta, fblk, xcol, sem_i, sem_r):
        return pltpu.make_async_remote_copy(
            src_ref=w1.at[hh],
            dst_ref=wf.at[
                pl.ds(pl.multiple_of(fblk * fb, fb), fb), pl.ds(pl.multiple_of(xcol * cb, cb), cb)
            ],
            send_sem=w2_ss.at[sem_i], recv_sem=w2_rs.at[sem_r],
            device_id=dev(hh, ty, rem(z + delta + nz, nz), tc), device_id_type=MESH,
        )

    def w2_sent(hh, delta):
        segment = div(rem(z + delta + nz, nz), nl)
        return (segment != hh) & jnp.logical_not(w2_self(hh, delta))

    def w2_send(hh):
        @pl.loop(0, nl)
        def _(dk):
            delta = w2_delta(hh, dk)

            @pl.when(w2_sent(hh, delta))
            def _():
                w2_copy(hh, delta, zl, x, hh * nl + dk, x * nl + zl).start()

    w2_send(h)
    for k in near_first:
        other = rem(h + nh - k, nh)
        w1_copy(k, other).wait_recv()
        w2_send(other)

    @pl.when((x != h) & untwisted)
    def _():
        wf[pl.ds(frow, fb), pl.ds(pl.multiple_of(x * cb, cb), cb)] = w1[x]

    @pl.loop(1, nsame)
    def _(k):
        i = rem(me_same - k + nsame, nsame)
        p = of_core(i, c)
        d_whole(p, p, sibling).wait_recv()
        d_forward(i, p).start()

    @pl.loop(0, nsame)
    def _(k):
        p = of_core(rem(me_same - k + nsame, nsame), 1 - c)
        d_scaled(p, p, sibling).wait_recv()

    @pl.loop(0, nsame)
    def _(i):
        d_forward(i, of_core(i, 1 - c)).wait_recv()

    def chain_copy(long, a, t):
        toward = way if long else -way
        d = (steps if long else steps - 1) - t
        slot, ss, rs = (lng, lg_ss, lg_rs) if long else (sht, sh_ss, sh_rs)
        return pltpu.make_async_remote_copy(
            src_ref=tsnd.at[a, rem(zl + toward * d + nl, nl)], dst_ref=slot.at[a, t],
            send_sem=ss.at[a, t], recv_sem=rs.at[a, t],
            device_id=dev(x, y, rem(z + toward + nz, nz), c), device_id_type=MESH,
        )

    def chain_step(t):
        for a in range(2):
            for long in (True, False):
                length = steps if long else steps - 1
                if t < length:
                    toward = way if long else -way
                    piece = rem(zl + toward * (length - t) + nl, nl)
                    slot = lng if long else sht
                    chain_copy(long, a, t - 1).wait_recv()
                    both = tsnd[a, piece].astype(F32) + slot[a, t - 1].astype(F32)
                    tsnd[a, piece] = both.astype(BF)
                    chain_copy(long, a, t).start()

    fchunk = div(fdim, 2)
    for a in range(2):
        lanes = slice(fdim + a * hc, fdim + (a + 1) * hc)
        sc_a = rcv[:, :, lanes].reshape(npl * cap, hc)
        for k in range(2):
            hid_c = rcv[:, :, k * fchunk:(k + 1) * fchunk].reshape(npl * cap, fchunk)
            t = dot(hid_c, sc_a, ((0,), (0,))).astype(BF)
            tsnd[a, k * div(nl, 2):(k + 1) * div(nl, 2)] = t.reshape(div(nl, 2), fb, hc)
        chain_copy(True, a, 0).start()
        if steps > 1:
            chain_copy(False, a, 0).start()

    def weights_arrived():
        @pl.when(x == h)
        def _():
            @pl.loop(0, nx)
            def _(i):
                @pl.when(jnp.logical_not(untwisted & (i == x)))
                def _():
                    wo_copy(i).wait_recv()

        @pl.when(x != h)
        def _():
            @pl.loop(0, nx * nl)
            def _(i):
                @pl.when(jnp.logical_not(untwisted & (i == x * nl + zl)))
                def _():
                    w2_copy(0, 0, rem(i, nl), div(i, nl), i, i).wait_recv()

    def x_copy(k):
        return pltpu.make_async_remote_copy(
            src_ref=xb_snd.at[k], dst_ref=xb_rcv.at[k],
            send_sem=x_ss.at[k], recv_sem=x_rs.at[k],
            device_id=sibling, device_id_type=MESH,
        )

    def r_whole(p, slot, target=None):
        return pltpu.make_async_remote_copy(
            src_ref=ret_snd.at[p], dst_ref=ret_rcv.at[slot],
            send_sem=r_ss.at[p], recv_sem=r_rs.at[slot],
            device_id=target or plane(p), device_id_type=MESH,
        )

    def r_out(p, slot, target=None):
        return pltpu.make_async_remote_copy(
            src_ref=ret_snd.at[p, :, pl.ds(0, dc)], dst_ref=ret_rcv.at[slot, :, pl.ds(0, dc)],
            send_sem=r_ss.at[p], recv_sem=r_rs.at[slot],
            device_id=target or plane(p), device_id_type=MESH,
        )

    def far_out(k):
        p0 = (2 * k + 1 - c) * ne
        hid_c = rcv[pl.ds(p0, ne), :, 0:fdim].reshape(ne * cap, fdim)
        o = dot(hid_c, wf[...], ((1,), (0,))).astype(BF)
        ret_snd[pl.ds(p0, ne), :, 0:dc] = o.reshape(ne, cap, dc)

        @pl.loop(0, ne)
        def _(i):
            r_out(p0 + rem(me + i, ne), me).start()

    def far_back(k):
        p0 = (2 * k + 1 - c) * ne
        sc_c = rcv[pl.ds(p0, ne), :, fdim:fdim + dc].reshape(ne * cap, dc)
        b = dot(sc_c, wf[...], ((1,), (1,))).astype(BF)
        xb_snd[k] = b.reshape(ne, cap, fdim)
        x_copy(k).start()

    def near_rows(k):
        p0 = (2 * k + c) * ne
        hid_c = rcv[pl.ds(p0, ne), :, 0:fdim].reshape(ne * cap, fdim)
        sc_c = rcv[pl.ds(p0, ne), :, fdim:fdim + dc].reshape(ne * cap, dc)
        o = dot(hid_c, wf[...], ((1,), (0,))).astype(BF)
        ret_snd[pl.ds(p0, ne), :, 0:dc] = o.reshape(ne, cap, dc)
        b = dot(sc_c, wf[...], ((1,), (1,)))
        x_copy(k).wait_recv()
        b = b.reshape(ne, cap, fdim) + xb_rcv[k].astype(F32)
        ret_snd[pl.ds(p0, ne), :, dc:dc + fdim] = b.astype(BF)

        @pl.loop(0, ne)
        def _(i):
            p = p0 + rem(me + i, ne)

            @pl.when(p != me)
            def _():
                r_whole(p, me).start()

    def ga_copy(j, slot):
        return pltpu.make_async_remote_copy(
            src_ref=g2s.at[j], dst_ref=ga.at[slot],
            send_sem=ga_ss.at[j], recv_sem=ga_rs.at[slot],
            device_id=dev(j, ty, z, tc), device_id_type=MESH,
        )

    def gb_copy(j, slot):
        return pltpu.make_async_remote_copy(
            src_ref=ga.at[j], dst_ref=gb.at[slot],
            send_sem=gb_ss.at[j], recv_sem=gb_rs.at[slot],
            device_id=dev(x, y, j * nl + zl, c), device_id_type=MESH,
        )

    def chain_end():
        for a in range(2):
            total = tsnd[a, zl].astype(F32)
            chain_copy(True, a, steps - 1).wait_recv()
            total = total + lng[a, steps - 1].astype(F32)
            if steps > 1:
                chain_copy(False, a, steps - 2).wait_recv()
                total = total + sht[a, steps - 2].astype(F32)
            for i in range(div(nx, 2)):
                g2s[a * div(nx, 2) + i] = total[:, i * cb:(i + 1) * cb].astype(BF)

        @pl.loop(0, nx)
        def _(j):
            @pl.when(jnp.logical_not((j == x) & untwisted))
            def _():
                ga_copy(j, x).start()

        @pl.when(untwisted)
        def _():
            ga[x] = g2s[x]

    def along_z():
        @pl.loop(0, nx)
        def _(j):
            @pl.when(jnp.logical_not((j == x) & untwisted))
            def _():
                ga_copy(j, j).wait_recv()

            @pl.when(j != h)
            def _():
                gb_copy(j, h).start()

        gb[h] = ga[h]

    work = [functools.partial(chain_step, t) for t in range(1, steps)] + [chain_end, along_z]
    rows = [functools.partial(far_out, k) for k in range(nq)]
    rows += [functools.partial(far_back, k) for k in range(nq)]
    rows += [functools.partial(near_rows, k) for k in range(nq)]
    for step in work[:2] + [weights_arrived] + rows[:3] + work[2:3] + rows[3:4] + work[3:4] + rows[4:5] + work[4:] + rows[5:]:
        step()
    ret_rcv[me] = ret_snd[me]

    for k in range(1, nh):
        w1_copy(k, h).wait_send()

    @pl.when(jnp.logical_not((x == h) & untwisted))
    def _():
        wo_copy(x).wait_send()

    @pl.loop(0, nsame)
    def _(i):
        p, far = of_core(i, c), of_core(i, 1 - c)
        d_forward(i, p).wait_send()
        d_scaled(far, me, sibling).wait_send()

        @pl.when(p != me)
        def _():
            d_whole(p, me, sibling).wait_send()

    @pl.loop(0, nx * nl)
    def _(i):
        @pl.when(w2_sent(div(i, nl), w2_delta(div(i, nl), rem(i, nl))))
        def _():
            w2_copy(0, 0, 0, 0, i, 0).wait_send()

    for a in range(2):
        for t in range(steps):
            chain_copy(True, a, t).wait_send()
            if t < steps - 1:
                chain_copy(False, a, t).wait_send()

    @pl.loop(0, nsame)
    def _(k):
        p = of_core(rem(me_same - k + nsame, nsame), 1 - c)
        r_out(p, p, sibling).wait_recv()

    @pl.loop(1, nsame)
    def _(k):
        p = of_core(rem(me_same - k + nsame, nsame), c)
        r_whole(p, p, sibling).wait_recv()

    for q in range(ny):
        rows = ret_rcv[q * ne:(q + 1) * ne, :, 0:dc].reshape(ne * cap, dc)
        token_out = gate * dot(placing, rows, ((0,), (0,)))
        for xx in range(nx):
            s0 = (xx * ny + q) * cb
            mixed_ref[:, s0:s0 + cb] = token_out[:, xx * cb:(xx + 1) * cb].astype(BF)
    back = ret_rcv[pl.ds(c * ne, ne), :, dc:dc + fdim].astype(F32)
    for k in range(1, nq):
        back = back + ret_rcv[pl.ds((2 * k + c) * ne, ne), :, dc:dc + fdim].astype(F32)
    back = back.reshape(ne * cap, fdim).astype(BF)
    hg_ref[...] = dot(placing, back, ((0,), (0,))).astype(BF)

    @pl.loop(0, nh)
    def _(hs):
        @pl.when(hs != h)
        def _():
            gb_copy(0, hs).wait_recv()

    total = gb[0].astype(F32)
    for hs in range(1, nh):
        total = total + gb[hs].astype(F32)
    cg_ref[0] = total * scale

    @pl.loop(0, nsame)
    def _(i):
        p, far = of_core(i, c), of_core(i, 1 - c)
        r_out(far, me, sibling).wait_send()

        @pl.when(p != me)
        def _():
            r_whole(p, me, sibling).wait_send()

    @pl.loop(0, nq)
    def _(k):
        x_copy(k).wait_send()

    @pl.loop(0, nx)
    def _(j):
        @pl.when(jnp.logical_not((j == x) & untwisted))
        def _():
            ga_copy(j, x).wait_send()

        @pl.when(j != h)
        def _():
            gb_copy(j, h).wait_send()


def body(nl, nh, nx, ny, hidden_in, expert_ids, gate_prob, out_grad, codes, scales):
    tok, fdim = hidden_in.shape
    ddim = out_grad.shape[1]
    cb = codes.shape[2]
    dc = nx * cb
    ne = 2 * nx
    npl = ny * ne
    cap = 3 * tok // (2 * ne)
    fb = fdim // nl
    dma = pltpu.SemaphoreType.DMA
    vmem = pl.BlockSpec(memory_space=pltpu.VMEM)
    hbm = pl.BlockSpec(memory_space=pl.ANY)
    return pl.pallas_call(
        functools.partial(kernel, nl, nh, nx, ny),
        out_shape=(
            jax.ShapeDtypeStruct((tok, ddim), BF),
            jax.ShapeDtypeStruct((tok, fdim), BF),
            jax.ShapeDtypeStruct((1, fb, cb), F32),
        ),
        in_specs=[vmem, vmem, hbm, hbm, hbm, vmem],
        out_specs=(vmem,) * 3,
        scratch_shapes=[
            pltpu.VMEM((tok, fdim), BF),
            pltpu.VMEM((tok, ddim), BF),
            pltpu.VMEM((fdim, cb), BF),
            pltpu.VMEM((npl, cap, fdim + dc), BF),
            pltpu.VMEM((npl, cap, fdim + dc), BF),
            pltpu.VMEM((npl, cap, fdim + dc), BF),
            pltpu.VMEM((npl, cap, fdim + dc), BF),
            pltpu.VMEM((ny // 2, ne, cap, fdim), BF),
            pltpu.VMEM((ny // 2, ne, cap, fdim), BF),
            pltpu.VMEM((fdim, cb), BF),
            pltpu.VMEM((nh, fb, cb), BF),
            pltpu.VMEM((fdim, dc), BF),
            pltpu.VMEM((2, nl, fb, dc // 2), BF),
            pltpu.VMEM((2, nl // 2, fb, dc // 2), BF),
            pltpu.VMEM((2, nl // 2, fb, dc // 2), BF),
            pltpu.VMEM((nx, fb, cb), BF),
            pltpu.VMEM((nx, fb, cb), BF),
            pltpu.VMEM((nh, fb, cb), BF),
            dma((3,)), dma((npl,)), dma((npl,)), dma((npl // 2,)), dma((npl // 2,)),
            dma((npl,)), dma((npl,)), dma((ny // 2,)), dma((ny // 2,)),
            dma((nh,)), dma((nh,)), dma(()), dma((nx,)), dma((nx * nl,)), dma((nx * nl,)),
            dma((2, nl // 2)), dma((2, nl // 2)), dma((2, nl // 2)), dma((2, nl // 2)), dma((nx,)), dma((nx,)), dma((nx,)), dma((nh,)),
        ],
        compiler_params=pltpu.CompilerParams(
            collective_id=0, has_side_effects=True, vmem_limit_bytes=60 * 2**20
        ),
        cost_estimate=pl.CostEstimate(
            flops=6 * npl * cap * fdim * dc, bytes_accessed=4 * tok * ddim, transcendentals=0
        ),
    )(
        expert_ids.reshape(1, tok), gate_prob.reshape(1, tok), hidden_in, out_grad, codes, scales
    )


def solution(mesh):
    nl, nh = mesh.shape["rep"], mesh.shape["node"] // 2
    nx = nh
    ny = mesh.shape["shard"] // nx
    return jax.shard_map(
        functools.partial(body, nl, nh, nx, ny),
        mesh=mesh,
        in_specs=(
            P(("rep", "node", "shard"), None),
            P(("rep", "node", "shard"), None),
            P(("rep", "node", "shard")),
            P(("rep", "node", "shard"), None),
            P("node", None, "shard"),
            P("node", None),
        ),
        out_specs=(
            P(("rep", "node", "shard"), None),
            P(("rep", "node", "shard"), None),
            P("node", "rep", "shard"),
        ),
        check_vma=False,
    )
```

time: 106 us -> 97.4 us (0.919)
  the two profiles are of different devices: /device:TPU:49 before, /device:TPU:36 now
where the time goes in v3:
time: 97.4 us; the launch traced here: 97.2 us
  Pallas kernels  93.2 us (96%)
  local copies, waits for them, and re-layouts  3.34 us (3%)
    pallas_call x1, Pallas kernels, body(): pl.pallas_call(functools.partial(kernel, nl, nh, nx, ny), out_shape=(jax....  93.2 us
    unnamed x7, local copies, waits for them, and re-layouts  3.34 us

profile of v3, /device:TPU:36, one launch (start us, length us, event | category | flops | bytes accessed | tf_op | source)
XLA Modules:
  0.0 97.2 jit_solution(662242028980712837)
XLA Ops:
  0.6 93.2 %shard_map.85 = (bf16[128,2048]{1,0:T(8,128)(2,1)}, bf16[128,768]{1,0:T(8,128)(2,1)}, f32[1,96,128]{2,1,0:T(8,128)}) custom-call(s32[1,128]{1,0:T(1,128)} %bitcast.2, f32[1,128]{1,0:T(1,128)} %bitcast.3, bf16[128,768]{1,0:T(8,128)(2,1)} %hid_hbm.1, bf16[128,2048]{1,0:T(8,128)(2,1)} %og_hbm.1, bf16[1,768,128]{2,1,0:T(8,128)(2,1)} %codes_hbm.1, ...), custom_call_target="tpu_custom_call" | custom-call | flops 1811939328 | bytes 1048576 | tf_op jit(solution)/shard_map/pallas_call | solution.py:531
  93.8 0.0 copy-start
  93.9 1.9 %copy.12 = bf16[128,2048]{1,0:T(8,128)(2,1)} copy(bf16[128,2048]{1,0:T(8,128)(2,1)} %get-tuple-element.6) | data formatting | bytes 1048576
  95.8 0.0 copy-done
  95.8 0.0 copy-start.1
  95.8 0.7 copy.13
  96.5 0.1 copy-done.1
  96.6 0.6 copy.14
Async XLA Ops:
  93.8 1.9 %copy-start = (bf16[128,768]{1,0:T(8,128)(2,1)S(1)}, bf16[128,768]{1,0:T(8,128)(2,1)}, u32[]{:S(2)}) copy-start(bf16[128,768]{1,0:T(8,128)(2,1)} %get-tuple-element.7) | copy-start | bytes 589828
  95.8 0.8 copy-start.1

commit v4 on v3

--- a/solution.py
+++ b/solution.py
@@ -30,7 +30,7 @@
     mixed_ref, hg_ref, cg_ref,
     hid_ref, og_ref, codes_ref,
     snd, rcv, ret_snd, ret_rcv, xb_snd, xb_rcv, wown, w1, wf, tsnd, lng, sht, g2s, ga, gb,
-    in_s, d_ss, d_rs, f_ss, f_rs, r_ss, r_rs, x_ss, x_rs,
+    in_s, d_ss, d_rs, f_ss, f_rs, r_ss, r_rs, rb_ss, rb_rs, x_ss, x_rs,
     w1_ss, w1_rs, wo_ss, wo_rs, w2_ss, w2_rs, lg_ss, lg_rs, sh_ss, sh_rs, ga_ss, ga_rs, gb_ss, gb_rs,
 ):
     ne = 2 * nx
@@ -324,10 +324,10 @@
             device_id=sibling, device_id_type=MESH,
         )
 
-    def r_whole(p, slot, target=None):
-        return pltpu.make_async_remote_copy(
-            src_ref=ret_snd.at[p], dst_ref=ret_rcv.at[slot],
-            send_sem=r_ss.at[p], recv_sem=r_rs.at[slot],
+    def r_back(p, slot, target=None):
+        return pltpu.make_async_remote_copy(
+            src_ref=ret_snd.at[p, :, pl.ds(dc, fdim)], dst_ref=ret_rcv.at[slot, :, pl.ds(dc, fdim)],
+            send_sem=rb_ss.at[p], recv_sem=rb_rs.at[slot],
             device_id=target or plane(p), device_id_type=MESH,
         )
 
@@ -355,12 +355,23 @@
         xb_snd[k] = b.reshape(ne, cap, fdim)
         x_copy(k).start()
 
-    def near_rows(k):
+    def near_out(k):
         p0 = (2 * k + c) * ne
         hid_c = rcv[pl.ds(p0, ne), :, 0:fdim].reshape(ne * cap, fdim)
-        sc_c = rcv[pl.ds(p0, ne), :, fdim:fdim + dc].reshape(ne * cap, dc)
         o = dot(hid_c, wf[...], ((1,), (0,))).astype(BF)
         ret_snd[pl.ds(p0, ne), :, 0:dc] = o.reshape(ne, cap, dc)
+
+        @pl.loop(0, ne)
+        def _(i):
+            p = p0 + rem(me + i, ne)
+
+            @pl.when(p != me)
+            def _():
+                r_out(p, me).start()
+
+    def near_back(k):
+        p0 = (2 * k + c) * ne
+        sc_c = rcv[pl.ds(p0, ne), :, fdim:fdim + dc].reshape(ne * cap, dc)
         b = dot(sc_c, wf[...], ((1,), (1,)))
         x_copy(k).wait_recv()
         b = b.reshape(ne, cap, fdim) + xb_rcv[k].astype(F32)
@@ -372,7 +383,7 @@
 
             @pl.when(p != me)
             def _():
-                r_whole(p, me).start()
+                r_back(p, me).start()
 
     def ga_copy(j, slot):
         return pltpu.make_async_remote_copy(
@@ -425,8 +436,10 @@
     work = [functools.partial(chain_step, t) for t in range(1, steps)] + [chain_end, along_z]
     rows = [functools.partial(far_out, k) for k in range(nq)]
     rows += [functools.partial(far_back, k) for k in range(nq)]
-    rows += [functools.partial(near_rows, k) for k in range(nq)]
-    for step in work[:2] + [weights_arrived] + rows[:3] + work[2:3] + rows[3:4] + work[3:4] + rows[4:5] + work[4:] + rows[5:]:
+    rows += [functools.partial(near_out, k) for k in range(nq)]
+    rows += [functools.partial(near_back, k) for k in range(nq)]
+    order = work[:2] + [weights_arrived] + rows[:3] + work[2:3] + rows[3:4]
+    for step in order + work[3:4] + rows[4:6] + work[4:] + rows[6:]:
         step()
     ret_rcv[me] = ret_snd[me]
 
@@ -467,7 +480,8 @@
     @pl.loop(1, nsame)
     def _(k):
         p = of_core(rem(me_same - k + nsame, nsame), c)
-        r_whole(p, p, sibling).wait_recv()
+        r_out(p, p, sibling).wait_recv()
+        r_back(p, p, sibling).wait_recv()
 
     for q in range(ny):
         rows = ret_rcv[q * ne:(q + 1) * ne, :, 0:dc].reshape(ne * cap, dc)
@@ -499,7 +513,8 @@
 
         @pl.when(p != me)
         def _():
-            r_whole(p, me, sibling).wait_send()
+            r_out(p, me, sibling).wait_send()
+            r_back(p, me, sibling).wait_send()
 
     @pl.loop(0, nq)
     def _(k):
@@ -557,7 +572,7 @@
             pltpu.VMEM((nx, fb, cb), BF),
             pltpu.VMEM((nh, fb, cb), BF),
             dma((3,)), dma((npl,)), dma((npl,)), dma((npl // 2,)), dma((npl // 2,)),
-            dma((npl,)), dma((npl,)), dma((ny // 2,)), dma((ny // 2,)),
+            dma((npl,)), dma((npl,)), dma((npl,)), dma((npl,)), dma((ny // 2,)), dma((ny // 2,)),
             dma((nh,)), dma((nh,)), dma(()), dma((nx,)), dma((nx * nl,)), dma((nx * nl,)),
             dma((2, nl // 2)), dma((2, nl // 2)), dma((2, nl // 2)), dma((2, nl // 2)), dma((nx,)), dma((nx,)), dma((nx,)), dma((nh,)),
         ],

time: 97.4 us -> 97.9 us (level)
  no operation moved by 1% of the time
where the time goes in v4:
time: 97.9 us; the launch traced here: 97.5 us
  Pallas kernels  93.5 us (96%)
  local copies, waits for them, and re-layouts  3.34 us (3%)
    pallas_call x1, Pallas kernels, body(): pl.pallas_call(functools.partial(kernel, nl, nh, nx, ny), out_shape=(jax....  93.5 us
    unnamed x7, local copies, waits for them, and re-layouts  3.34 us

profile of v4, /device:TPU:36, one launch (start us, length us, event | category | flops | bytes accessed | tf_op | source)
XLA Modules:
  0.0 97.5 jit_solution(13146085094091243302)
XLA Ops:
  0.6 93.5 %shard_map.85 = (bf16[128,2048]{1,0:T(8,128)(2,1)}, bf16[128,768]{1,0:T(8,128)(2,1)}, f32[1,96,128]{2,1,0:T(8,128)}) custom-call(s32[1,128]{1,0:T(1,128)} %bitcast.2, f32[1,128]{1,0:T(1,128)} %bitcast.3, bf16[128,768]{1,0:T(8,128)(2,1)} %hid_hbm.1, bf16[128,2048]{1,0:T(8,128)(2,1)} %og_hbm.1, bf16[1,768,128]{2,1,0:T(8,128)(2,1)} %codes_hbm.1, ...), custom_call_target="tpu_custom_call" | custom-call | flops 1811939328 | bytes 1048576 | tf_op jit(solution)/shard_map/pallas_call | solution.py:546
  94.2 0.0 copy-start
  94.2 1.9 %copy.12 = bf16[128,2048]{1,0:T(8,128)(2,1)} copy(bf16[128,2048]{1,0:T(8,128)(2,1)} %get-tuple-element.6) | data formatting | bytes 1048576
  96.1 0.0 copy-done
  96.1 0.0 copy-start.1
  96.1 0.7 copy.13
  96.8 0.1 copy-done.1
  96.9 0.6 copy.14
Async XLA Ops:
  94.2 1.9 %copy-start = (bf16[128,768]{1,0:T(8,128)(2,1)S(1)}, bf16[128,768]{1,0:T(8,128)(2,1)}, u32[]{:S(2)}) copy-start(bf16[128,768]{1,0:T(8,128)(2,1)} %get-tuple-element.7) | copy-start | bytes 589828
  96.1 0.8 copy-start.1
